TPU v7x, 32 devices: a whole 2x2x4 slice. The times are simulated.
32 devices in a mesh: dp: 4 (over y, core), expert: 8 (over z, x).
Axes of the slice: x: 2, y: 2, z: 4, core: 2. Of those that a mesh axis runs over, the one named last changes fastest.
Arguments:
- tokens: bfloat16 [8192, 2048], P(('dp', 'expert')), parts along dimension 0, may hold values from -6 to 6
- target: int32 [8192, 8], P(('dp', 'expert')), parts along dimension 0, may hold values from 0 to 23, as said below
- router_weight: float32 [8192, 8], P(('dp', 'expert')), parts along dimension 0, may hold values from 0.1 to 1
- replica_pick: int32 [32], P(('dp', 'expert')), parts along dimension 0, may hold values from 0 to 1
- w_gate: bfloat16 [16, 2048, 768], P('expert'), may hold values from -0.125 to 0.125
- w_up: bfloat16 [16, 2048, 768], P('expert'), may hold values from -0.125 to 0.125
- w_down: bfloat16 [16, 768, 2048], P('expert'), may hold values from -0.21875 to 0.21875
Outputs:
- mixed: bfloat16 [8192, 2048], P(('dp', 'expert')), parts along dimension 0
There are 4 independent parts, one for each index of `dp`. A program takes and returns all parts, laid end to end along the dimension named above; an argument that names none is the same for every part. Nothing has to cross between parts.
Inputs may be any that keep to these rules, and one draw needn't show every extreme that they name: `target`: within each aligned block of 256 rows (one device's tokens) no slot is named more than 128 times, and at least one slot, the same one in every block, is named exactly 128 times in every block (other slots may also reach 128); the 8 slots of a row name 8 different experts.
All inputs are finite; a program needn't handle non-finite values.
Results may differ from a plain program's by a relative error of at most 0.008.
Values may be sent and summed in bfloat16 or wider, within the bound.
No kernel may reach another device: no remote copies, remote signals or barrier semaphores. Data moves between devices by JAX's collectives and lax.ppermute only.
A program may use at most 192 MiB of HBM per device.

v0:
```python
import jax
import jax.numpy as jnp
from jax import lax
from jax.sharding import PartitionSpec as P


def body(tokens, target, router_weight, replica_pick, w_gate, w_up, w_down):
    tok_rows, width = tokens.shape
    top = target.shape[1]
    per_device = w_gate.shape[0]
    slots = per_device + 1
    groups = lax.axis_size("expert")
    virtual = groups * slots
    capacity = 3 * tok_rows * top // (2 * virtual)
    flat = target.reshape(-1)
    onehot = (flat[:, None] == jnp.arange(virtual, dtype=jnp.int32)[None, :]).astype(jnp.int32)
    earlier = jnp.cumsum(onehot, axis=0) - onehot
    place = jnp.sum(earlier * onehot, axis=1)
    row_index = flat * capacity + place
    buffer = jnp.zeros((virtual * capacity, width), jnp.bfloat16)
    buffer = buffer.at[row_index].set(jnp.repeat(tokens, top, axis=0), unique_indices=True)
    outgoing = buffer.reshape(groups, slots, capacity, width)
    lent = replica_pick[0]
    own_gate = lax.dynamic_index_in_dim(w_gate, lent, 0, keepdims=False)
    own_up = lax.dynamic_index_in_dim(w_up, lent, 0, keepdims=False)
    own_down = lax.dynamic_index_in_dim(w_down, lent, 0, keepdims=False)
    spare_gate, spare_up, spare_down = (own_gate, own_up, own_down)
    outgoing = outgoing.at[:, per_device].set(jnp.roll(outgoing[:, per_device], -1, axis=0))
    rows = lax.all_to_all(outgoing, "expert", split_axis=0, concat_axis=0, tiled=True)
    owned = rows[:, :per_device]
    gate = jnp.einsum("nscd,sdf->nscf", owned, w_gate, preferred_element_type=jnp.float32)
    upper = jnp.einsum("nscd,sdf->nscf", owned, w_up, preferred_element_type=jnp.float32)
    hidden = (jax.nn.silu(gate) * upper).astype(jnp.bfloat16)
    result = jnp.einsum(
        "nscf,sfd->nscd", hidden, w_down, preferred_element_type=jnp.float32
    ).astype(jnp.bfloat16)
    spare_rows = rows[:, per_device]
    gate_two = jnp.einsum("ncd,df->ncf", spare_rows, spare_gate, preferred_element_type=jnp.float32)
    upper_two = jnp.einsum("ncd,df->ncf", spare_rows, spare_up, preferred_element_type=jnp.float32)
    hidden_two = (jax.nn.silu(gate_two) * upper_two).astype(jnp.bfloat16)
    result_two = jnp.einsum(
        "ncf,fd->ncd", hidden_two, spare_down, preferred_element_type=jnp.float32
    ).astype(jnp.bfloat16)
    results = jnp.concatenate([result, result_two[:, None]], axis=1)
    returned = lax.all_to_all(results, "expert", split_axis=0, concat_axis=0, tiled=True)
    returned = returned.at[:, per_device].set(jnp.roll(returned[:, per_device], 1, axis=0))
    picked = returned.reshape(virtual * capacity, width)[row_index].reshape(tok_rows, top, width)
    share = router_weight / jnp.sum(router_weight, axis=1, keepdims=True)
    mixed = jnp.sum(share[:, :, None] * picked.astype(jnp.float32), axis=1)
    return mixed.astype(jnp.bfloat16)


def solution(mesh):
    in_specs = (
        P(("dp", "expert"), None),
        P(("dp", "expert"), None),
        P(("dp", "expert"), None),
        P(("dp", "expert")),
        P("expert", None, None),
        P("expert", None, None),
        P("expert", None, None),
    )
    out_specs = P(("dp", "expert"), None)
    return jax.shard_map(body, mesh=mesh, in_specs=in_specs, out_specs=out_specs, check_vma=False)
```

profile of v0, /device:TPU:0, one launch (start us, length us, event | category | flops | bytes accessed | tf_op | source)
XLA Modules:
  0.0 708.7 jit_solution(4945600549022467109)
XLA Ops:
  0.0 0.9 copy.22
  0.9 0.1 eq.29
  1.0 0.1 eq.25
  1.1 0.7 broadcast_multiply_fusion
  1.9 6.8 reduce-window.6
  8.7 0.1 slice.110
  8.8 0.2 copy.33
  9.0 0.2 reduce-window.9
  9.2 0.1 broadcast_add_fusion
  9.3 0.1 copy.21
  9.4 0.1 mul.44
  9.6 0.1 fusion.38
  9.7 19.0 %scatter_custom_fusion = bf16[3072,2048]{1,0:T(8,128)(2,1)} fusion(s32[2048]{0:T(1024)S(1)} %bitcast.128, bf16[]{:T(256)} %constant.72.clone.1, bf16[256,2048]{1,0:T(8,128)(2,1)S(1)} %copy-done), kind=kCustom, calls=%fused_computation.5 | custom fusion | bytes 13631490 | tf_op jit(solution)/shard_map/scatter | solution.py:21
  28.7 2.3 slice_bitcast_fusion.4
  31.0 1.1 slice_bitcast_fusion.10
  32.1 2.4 fusion.18
  34.5 7.6 %all-to-all-start = ((bf16[8,3,128,2048]{3,2,1,0:T(8,128)(2,1)}), bf16[8,3,128,2048]{3,2,1,0:T(8,128)(2,1)}, u32[]{:S(2)}, u32[]{:S(2)}) async-start(bf16[8,3,128,2048]{3,2,1,0:T(8,128)(2,1)} %fusion.18), calls=%async_computation | async-start | bytes 25165824 | tf_op jit(solution)/shard_map/all_to_all | solution.py:29
  42.7 272.3 %all-to-all-done = bf16[8,3,128,2048]{3,2,1,0:T(8,128)(2,1)} async-done(((bf16[8,3,128,2048]{3,2,1,0:T(8,128)(2,1)}), bf16[8,3,128,2048]{3,2,1,0:T(8,128)(2,1)}, u32[]{:S(2)}, u32[]{:S(2)}) %all-to-all-start) | async-done | bytes 12582944 | tf_op jit(solution)/shard_map/all_to_all | solution.py:29
  315.0 12.6 %fusion.3 = f32[2,8,128,768]{3,2,1,0:T(8,128)} fusion(bf16[2,2048,768]{2,1,0:T(8,128)(2,1)} %param.16, bf16[8,3,128,2048]{3,2,1,0:T(8,128)(2,1)} %all-to-all-done), kind=kOutput, calls=%fused_computation.8 | convolution fusion | flops 6442450944 | bytes 20971520 | tf_op jit(solution)/shard_map/nscd,sdf->nscf/dot_general | solution.py:32
  327.6 8.2 %fusion.22 = f32[8,128,768]{2,1,0:T(8,128)} fusion(bf16[8,3,128,2048]{3,2,1,0:T(8,128)(2,1)} %all-to-all-done, bf16[2,2048,768]{2,1,0:T(8,128)(2,1)} %param.15, s32[]{:T(128)S(6)} %select_n.19), kind=kOutput, calls=%fused_computation.32 | convolution fusion | flops 3221225472 | bytes 10485764 | tf_op jit(solution)/shard_map/ncd,df->ncf/dot_general | solution.py:38
  335.8 13.2 %convert_bitcast_fusion.1 = bf16[8,1,128,2048]{3,2,0,1:T(8,128)(2,1)} fusion(bf16[2,768,2048]{2,1,0:T(8,128)(2,1)} %param.17, s32[]{:T(128)S(6)} %select_n.19, f32[8,128,768]{2,1,0:T(8,128)} %fusion.22, bf16[2,2048,768]{2,1,0:T(8,128)(2,1)} %param.16, bf16[8,3,128,2048]{3,2,1,0:T(8,128)(2,1)} %all-to-all-done), kind=kOutput, calls=%fused_computation.29 | convolution fusion | flops 6449266688 | bytes 17826816 | tf_op jit(solution)/shard_map/ncf,fd->ncd/dot_general | solution.py:41
  349.0 22.2 %convert_bitcast_fusion = bf16[8,2,128,2048]{3,2,0,1:T(8,128)(2,1)} fusion(bf16[2,768,2048]{2,1,0:T(8,128)(2,1)} %param.17, f32[2,8,128,768]{3,2,1,0:T(8,128)} %fusion.3, bf16[2,2048,768]{2,1,0:T(8,128)(2,1)} %param.15, bf16[8,3,128,2048]{3,2,1,0:T(8,128)(2,1)} %all-to-all-done), kind=kOutput, calls=%fused_computation.7 | convolution fusion | flops 12898533376 | bytes 35651584 | tf_op jit(solution)/shard_map/nscf,sfd->nscd/dot_general | solution.py:34
  371.2 5.4 pad_maximum_fusion
  376.6 5.2 copy.28
  381.8 13.8 %all-to-all-start.1 = ((bf16[8,3,128,2048]{3,2,1,0:T(8,128)(2,1)}), bf16[8,3,128,2048]{3,2,1,0:T(8,128)(2,1)}, u32[]{:S(2)}, u32[]{:S(2)}) async-start(bf16[8,3,128,2048]{3,2,1,0:T(8,128)(2,1)} %copy.28), calls=%async_computation.1 | async-start | bytes 25165824 | tf_op jit(solution)/shard_map/all_to_all | solution.py:45
  395.7 0.1 copy.20
  395.8 271.6 %all-to-all-done.1 = bf16[8,3,128,2048]{3,2,1,0:T(8,128)(2,1)} async-done(((bf16[8,3,128,2048]{3,2,1,0:T(8,128)(2,1)}), bf16[8,3,128,2048]{3,2,1,0:T(8,128)(2,1)}, u32[]{:S(2)}, u32[]{:S(2)}) %all-to-all-start.1) | async-done | bytes 12582944 | tf_op jit(solution)/shard_map/all_to_all | solution.py:45
  667.4 2.5 slice_bitcast_fusion.3
  669.9 1.1 slice_bitcast_fusion.9
  671.0 2.6 fusion.19
  673.7 22.6 %gather_fusion = bf16[2048,2048]{1,0:T(8,128)(2,1)} fusion(bf16[3072,2048]{1,0:T(8,128)(2,1)} %bitcast.31, s32[2048]{0:T(1024)S(1)} %broadcast_clamp_fusion), kind=kCustom, calls=%fused_computation | custom fusion | bytes 16785408 | tf_op jit(solution)/shard_map/gather | solution.py:47
  696.3 12.2 %fusion = bf16[256,2048]{1,0:T(8,128)(2,1)} fusion(bf16[2048,2048]{1,0:T(8,128)(2,1)} %gather_fusion, f32[256,8]{1,0:T(8,128)S(1)} %copy.20), kind=kLoop, calls=%fused_computation.3 | loop fusion | flops 12058624 | bytes 9445376 | tf_op jit(solution)/shard_map/reduce_sum | solution.py:49
  (11 shorter events, 0.1 us)
Async XLA Ops:
  0.0 9.7 %copy-start = (bf16[256,2048]{1,0:T(8,128)(2,1)S(1)}, bf16[256,2048]{1,0:T(8,128)(2,1)}, u32[]{:S(2)}) copy-start(bf16[256,2048]{1,0:T(8,128)(2,1)} %param.11) | copy-start | bytes 3145732
  34.5 280.5 %all-to-all-start = ((bf16[8,3,128,2048]{3,2,1,0:T(8,128)(2,1)}), bf16[8,3,128,2048]{3,2,1,0:T(8,128)(2,1)}, u32[]{:S(2)}, u32[]{:S(2)}) async-start(bf16[8,3,128,2048]{3,2,1,0:T(8,128)(2,1)} %fusion.18), calls=%async_computation | async-start | bytes 25165824 | tf_op jit(solution)/shard_map/all_to_all | solution.py:29
  381.8 13.8 %copy-start.2 = (f32[256,8]{0,1:T(8,128)S(1)}, f32[256,8]{0,1:T(8,128)}, u32[]{:S(2)}) copy-start(f32[256,8]{0,1:T(8,128)} %param.13) | copy-start | bytes 24580
  381.8 285.7 %all-to-all-start.1 = ((bf16[8,3,128,2048]{3,2,1,0:T(8,128)(2,1)}), bf16[8,3,128,2048]{3,2,1,0:T(8,128)(2,1)}, u32[]{:S(2)}, u32[]{:S(2)}) async-start(bf16[8,3,128,2048]{3,2,1,0:T(8,128)(2,1)} %copy.28), calls=%async_computation.1 | async-start | bytes 25165824 | tf_op jit(solution)/shard_map/all_to_all | solution.py:45
  673.7 34.9 %copy-start.1 = (bf16[256,2048]{1,0:T(8,128)(2,1)S(1)}, bf16[256,2048]{1,0:T(8,128)(2,1)}, u32[]{:S(2)}) copy-start(bf16[256,2048]{1,0:T(8,128)(2,1)} %param.11) | copy-start | bytes 3145732
where the time goes:
time: 718 us; the launch traced here: 709 us
  waiting for transfers between devices  544 us (76%)
  matrix products  56.2 us (8%)
  local copies, waits for them, and re-layouts  55.5 us (8%)
  other arithmetic  30.7 us (4%)
  starting transfers between devices  21.4 us (3%)
    all_to_all x1, waiting for transfers between devices, body(): lax.all_to_all(outgoing, 'expert', split_axis=0, concat_axis=0, tiled=True)  272 us
    all_to_all x1, waiting for transfers between devices, body(): lax.all_to_all(results, 'expert', split_axis=0, concat_axis=0, tiled=True)  272 us
    gather x1, local copies, waits for them, and re-layouts, body(): returned.reshape(virtual * capacity, width)[row_index]  22.6 us
    dot_general x1, matrix products, body(): jnp.einsum('nscf,sfd->nscd', hidden, w_down, preferred_element_type=jnp.f...  22.2 us
    scatter x1, local copies, waits for them, and re-layouts, body(): buffer.at[row_index]  19 us
  transfers between devices with their start and end apart: 2, of which 2 were waited for; matrix products, arithmetic and copies ran while one was open for 0% of the time, Pallas kernels for 0%

commit v1 on v0

v1 whole, which is shorter than its diff:
```python
import functools

import jax
import jax.numpy as jnp
from jax import lax
from jax.experimental import pallas as pl
from jax.experimental.pallas import tpu as pltpu
from jax.sharding import PartitionSpec as P


def ring_order(groups):
    columns = 1 << ((groups.bit_length() - 1) // 2)
    rows = groups // columns
    walk = [z * columns for z in range(rows)]
    for turn, z in enumerate(reversed(range(rows))):
        row = [z * columns + x for x in range(1, columns)]
        walk += row if turn % 2 == 0 else row[::-1]
    return walk


def expert_kernel(tiles, count, *refs):
    chunks = refs[:count]
    coeff_ref, gate_ref, up_ref, down_ref = refs[count:count + 4]
    outs = refs[count + 4:2 * count + 4]
    rows_ref, total_ref = refs[2 * count + 4:]
    step = pl.program_id(0)
    height = chunks[0].shape[0]

    @pl.when(step == 0)
    def _():
        for i in range(count):
            rows_ref[i * height:(i + 1) * height, :] = chunks[i][...]

    x = rows_ref[...]
    gate = jnp.dot(x, gate_ref[0], preferred_element_type=jnp.float32)
    upper = jnp.dot(x, up_ref[0], preferred_element_type=jnp.float32)
    coeff = coeff_ref[...]
    lane = lax.broadcasted_iota(jnp.int32, coeff.shape, 1)
    share = jnp.sum(jnp.where(lane == step // tiles, coeff, 0.0), axis=1, keepdims=True)
    hidden = (gate / (1.0 + jnp.exp(-gate)) * upper * share).astype(jnp.bfloat16)
    part = jnp.dot(hidden, down_ref[0], preferred_element_type=jnp.float32)

    @pl.when(step == 0)
    def _():
        total_ref[...] = part

    @pl.when(step > 0)
    def _():
        total_ref[...] += part

    @pl.when(step == pl.num_programs(0) - 1)
    def _():
        for i in range(count):
            outs[i][...] = total_ref[i * height:(i + 1) * height, :].astype(outs[i].dtype)


def experts(chunks, coeffs, w_gate, w_up, w_down):
    count = len(chunks)
    height, width = chunks[0].shape
    owned, unused, units = w_gate.shape
    tile = 256 if units % 256 == 0 else units
    tiles = units // tile
    rows = count * height
    coeff = jnp.concatenate(coeffs, axis=0) if count > 1 else coeffs[0]
    whole = pl.BlockSpec((height, width), lambda j: (0, 0))
    flops = 6 * rows * width * units * owned
    moved = 2 * 3 * owned * width * units + 4 * rows * width
    return pl.pallas_call(
        functools.partial(expert_kernel, tiles, count),
        grid=(owned * tiles,),
        in_specs=[whole] * count + [
            pl.BlockSpec((rows, coeff.shape[1]), lambda j: (0, 0)),
            pl.BlockSpec((1, width, tile), lambda j: (j // tiles, 0, j % tiles)),
            pl.BlockSpec((1, width, tile), lambda j: (j // tiles, 0, j % tiles)),
            pl.BlockSpec((1, tile, width), lambda j: (j // tiles, j % tiles, 0)),
        ],
        out_specs=[whole] * count,
        out_shape=[jax.ShapeDtypeStruct((height, width), jnp.bfloat16)] * count,
        scratch_shapes=[pltpu.VMEM((rows, width), jnp.bfloat16), pltpu.VMEM((rows, width), jnp.float32)],
        compiler_params=pltpu.CompilerParams(vmem_limit_bytes=48 * 1024 * 1024),
        cost_estimate=pl.CostEstimate(flops=flops, bytes_accessed=moved, transcendentals=rows * units * owned),
    )(*chunks, coeff, w_gate, w_up, w_down)


def body(tokens, target, router_weight, replica_pick, w_gate, w_up, w_down):
    height, width = tokens.shape
    owned = w_gate.shape[0]
    slots = owned + 1
    groups = lax.axis_size("expert")
    me = lax.axis_index("expert")
    walk = ring_order(groups)
    place = [walk.index(i) for i in range(groups)]
    ahead = [(walk[i], walk[(i + 1) % groups]) for i in range(groups)]
    back = [(b, a) for a, b in ahead]
    position = jnp.asarray(place, jnp.int32)[me]
    order = jnp.asarray(walk, jnp.int32)

    share = router_weight / jnp.sum(router_weight, axis=1, keepdims=True)
    label = jnp.arange(groups * slots, dtype=jnp.int32)
    table = jnp.sum(jnp.where(target.T[None, :, :] == label[:, None, None], share.T[None, :, :], 0.0), axis=1)
    tables = lax.all_gather(table, "expert", axis=0, tiled=False)
    mine = lax.dynamic_slice_in_dim(tables, me * slots, owned, axis=1)
    lent = lax.dynamic_index_in_dim(tables, lax.rem(me + 1, groups) * slots + owned, 1, keepdims=True)
    which = lax.broadcasted_iota(jnp.int32, (1, owned, 1), 1)
    coeffs = jnp.swapaxes(mine + jnp.where(which == replica_pick[0], lent, 0.0), 1, 2)

    def coeff(offset):
        owner = order[lax.rem(position + offset + groups, groups)]
        return lax.dynamic_index_in_dim(coeffs, owner, 0, keepdims=False)

    run = functools.partial(experts, w_gate=w_gate, w_up=w_up, w_down=w_down)
    far = groups // 2
    half = height // 2
    from_left, from_right = tokens, tokens
    left_parts, right_parts = {}, {}
    for s in range(1, far):
        from_left = lax.ppermute(from_left, "expert", ahead)
        from_right = lax.ppermute(from_right, "expert", back)
        if s == 1:
            own_part, = run([tokens], [coeff(0)])
        left_parts[s], right_parts[s] = run([from_left, from_right], [coeff(-s), coeff(s)])
    top_half = lax.ppermute(from_left[:half], "expert", ahead)
    low_half = lax.ppermute(from_right[half:], "expert", back)
    far_coeff = coeff(far)
    top_part, low_part = run([top_half, low_half], [far_coeff[:half], far_coeff[half:]])

    def add(a, b):
        return (a.astype(jnp.float32) + b.astype(jnp.float32)).astype(jnp.bfloat16)

    to_left = lax.ppermute(top_part, "expert", back)
    to_right = lax.ppermute(low_part, "expert", ahead)
    for s in range(far - 1, 0, -1):
        left, right = left_parts[s], right_parts[s]
        if s == far - 1:
            left = jnp.concatenate([add(left[:half], to_left), left[half:]], axis=0)
            right = jnp.concatenate([right[:half], add(right[half:], to_right)], axis=0)
        else:
            left, right = add(left, to_left), add(right, to_right)
        to_left = lax.ppermute(left, "expert", back)
        to_right = lax.ppermute(right, "expert", ahead)
    total = own_part.astype(jnp.float32) + to_left.astype(jnp.float32) + to_right.astype(jnp.float32)
    return total.astype(jnp.bfloat16)


def solution(mesh):
    in_specs = (
        P(("dp", "expert"), None),
        P(("dp", "expert"), None),
        P(("dp", "expert"), None),
        P(("dp", "expert")),
        P("expert", None, None),
        P("expert", None, None),
        P("expert", None, None),
    )
    out_specs = P(("dp", "expert"), None)
    return jax.shard_map(body, mesh=mesh, in_specs=in_specs, out_specs=out_specs, check_vma=False)
```

time: 718 us -> 233 us (0.32); the launches traced: 709 us -> 232 us
  waiting for transfers between devices: 544 us -> 78.5 us
  Pallas kernels: 0 us -> 70.6 us
  matrix products: 56.2 us -> 0 us
  local copies, waits for them, and re-layouts: 55.5 us -> 5.52 us
  blocking collectives: 0 us -> 30.9 us
  other arithmetic: 30.7 us -> 7.36 us
  between operations: 1 us -> 20.7 us
    all_to_all x2 -> x0, waiting for transfers between devices: 544 us -> none  [the longest x1 272 us: body(): lax.all_to_all(outgoing, 'expert', split_axis=0, concat_axis=0, tiled=True)]
    ppermute x0 -> x16, waiting for transfers between devices: none -> 78.5 us  [the longest x3 44 us: body(): from_left = lax.ppermute(from_left, 'expert', ahead)]
    pallas_call x0 -> x5, Pallas kernels: none -> 70.6 us  [experts(): pl.pallas_call(functools.partial(expert_kernel, tiles, count), grid=(owne...]
    dot_general x4 -> x0, matrix products: 56.2 us -> none  [the longest x1 22.2 us: body(): jnp.einsum('nscf,sfd->nscd', hidden, w_down, preferred_element_type=jnp.f...]
    all_gather x0 -> x1, blocking collectives: none -> 30.9 us  [body(): tables = lax.all_gather(table, 'expert', axis=0, tiled=False)]
    gather x1 -> x0, local copies, waits for them, and re-layouts: 22.6 us -> none  [body(): returned.reshape(virtual * capacity, width)[row_index]]
    all_to_all x2 -> x0, starting transfers between devices: 21.4 us -> none  [the longest x1 13.8 us: body(): lax.all_to_all(results, 'expert', split_axis=0, concat_axis=0, tiled=True)]
    scatter x1 -> x0, local copies, waits for them, and re-layouts: 19 us -> none  [body(): buffer.at[row_index]]
  transfers between devices with their start and end apart: 2 -> 16, of which waited for: 2 -> 9; matrix products, arithmetic and copies ran while one was open for 0% -> 4% of each run, Pallas kernels for 0% -> 26%
where the time goes in v1:
time: 233 us; the launch traced here: 232 us
  waiting for transfers between devices  78.5 us (34%)
  Pallas kernels  70.6 us (30%)
  blocking collectives  30.9 us (13%)
  between operations  20.7 us (9%)
  starting transfers between devices  18.3 us (8%)
  other arithmetic  7.36 us (3%)
  local copies, waits for them, and re-layouts  5.52 us (2%)
    pallas_call x5, Pallas kernels, experts(): pl.pallas_call(functools.partial(expert_kernel, tiles, count), grid=(owne...  70.6 us
    ppermute x3, waiting for transfers between devices, body(): from_left = lax.ppermute(from_left, 'expert', ahead)  44 us
    all_gather x1, blocking collectives, body(): tables = lax.all_gather(table, 'expert', axis=0, tiled=False)  30.9 us
    ppermute x3, waiting for transfers between devices, body(): to_right = lax.ppermute(right, 'expert', ahead)  13.2 us
    ppermute x1, waiting for transfers between devices, body(): to_right = lax.ppermute(low_part, 'expert', ahead)  12.5 us
    ppermute x1, waiting for transfers between devices, body(): top_half = lax.ppermute(from_left[:half], 'expert', ahead)  6.94 us
    ppermute x3, starting transfers between devices, body(): to_left = lax.ppermute(left, 'expert', back)  6.61 us
    ppermute x3, starting transfers between devices, body(): from_left = lax.ppermute(from_left, 'expert', ahead)  6.36 us
  transfers between devices with their start and end apart: 16, of which 9 were waited for; matrix products, arithmetic and copies ran while one was open for 4% of the time, Pallas kernels for 26%

profile of v1, /device:TPU:0, one launch (start us, length us, event | category | flops | bytes accessed | tf_op | source)
XLA Modules:
  0.0 231.9 jit_solution(12514989623097923344)
XLA Ops:
  0.0 3.0 %collective-permute-start = (bf16[256,2048]{1,0:T(8,128)(2,1)}, bf16[256,2048]{1,0:T(8,128)(2,1)S(1)}, u32[]{:S(2)}, u32[]{:S(2)}) collective-permute-start(bf16[256,2048]{1,0:T(8,128)(2,1)} %refs_0_.1), channel_id=1, source_target_pairs={{0,2},{2,4},{4,6},{6,7},{7,5},{5,3},{3,1},{1,0},{8,10},{10,12},{12... | collective-permute-start | bytes 3145736 | tf_op jit(solution)/shard_map/ppermute | solution.py:117
  3.0 23.3 %collective-permute-done.refs_0_ = bf16[256,2048]{1,0:T(8,128)(2,1)S(1)} collective-permute-done((bf16[256,2048]{1,0:T(8,128)(2,1)}, bf16[256,2048]{1,0:T(8,128)(2,1)S(1)}, u32[]{:S(2)}, u32[]{:S(2)}) %collective-permute-start) | collective-permute-done | bytes 1048608 | tf_op jit(solution)/shard_map/ppermute | solution.py:117
  26.3 1.8 collective-permute-start.2
  28.3 1.0 copy-done.1
  29.3 0.7 reduce_sum.18
  30.0 20.7 %collective-permute-done.2.refs_0_ = bf16[256,2048]{1,0:T(8,128)(2,1)} collective-permute-done((bf16[256,2048]{1,0:T(8,128)(2,1)S(1)}, bf16[256,2048]{1,0:T(8,128)(2,1)}, u32[]{:S(2)}, u32[]{:S(2)}) %collective-permute-start.2) | collective-permute-done | bytes 1048608 | tf_op jit(solution)/shard_map/ppermute | solution.py:117
  50.8 1.5 collective-permute-start.4
  52.3 0.5 collective-permute-start.5
  52.8 0.7 divide_bitcast_fusion
  53.5 1.2 dynamic_slice.61
  60.0 1.6 fusion
  71.3 0.8 select_reduce_fusion
  72.0 30.9 %all-gather = f32[192,256]{1,0:T(8,128)S(1)} all-gather(f32[24,256]{1,0:T(8,128)S(1)} %select_reduce_fusion), channel_id=2, replica_groups=mesh['dp'=4,'expert'=8] {'expert'}, dimensions={0}, use_global_device_ids=true | all-gather | bytes 221184 | tf_op jit(solution)/shard_map/all_gather | solution.py:101
  103.0 1.3 copy.26
  109.8 1.6 select_add_fusion
  111.7 2.1 collective-permute-start.7
  113.8 6.9 %collective-permute-done.6.refs_0_ = bf16[128,2048]{1,0:T(8,128)(2,1)S(1)} collective-permute-done((bf16[128,2048]{1,0:T(8,128)(2,1)S(1)}, bf16[128,2048]{1,0:T(8,128)(2,1)S(1)}, u32[]{:S(2)}, u32[]{:S(2)}) %collective-permute-start.6) | collective-permute-done | bytes 524320 | tf_op jit(solution)/shard_map/ppermute | solution.py:122
  120.9 11.3 %shard_map.95 = (bf16[128,2048]{1,0:T(8,128)(2,1)S(1)}, bf16[128,2048]{1,0:T(8,128)(2,1)S(1)}) custom-call(bf16[128,2048]{1,0:T(8,128)(2,1)S(1)} %collective-permute-done.6.refs_0_, bf16[128,2048]{1,0:T(8,128)(2,1)S(1)} %collective-permute-done.7.refs_1_, f32[256,2]{1,0:T(8,128)S(1)} %pad_maximum_fusion.5.refs_2_, bf16[2,2048,768]{2,1,0:T(8,128)(2,1)} %refs_3_.9, ...), custom_call_target="tpu_custom_call" | custom-call | flops 4831838208 | bytes 20971520 | tf_op jit(solution)/shard_map/pallas_call | solution.py:68
  132.2 2.1 collective-permute-start.8
  134.2 15.7 %shard_map.94 = (bf16[256,2048]{1,0:T(8,128)(2,1)S(1)}, bf16[256,2048]{1,0:T(8,128)(2,1)S(1)}) custom-call(bf16[256,2048]{1,0:T(8,128)(2,1)S(1)} %collective-permute-done.4.refs_0_, bf16[256,2048]{1,0:T(8,128)(2,1)S(1)} %collective-permute-done.5.refs_1_, f32[512,2]{1,0:T(8,128)S(1)} %pad_maximum_fusion.4.refs_2_, bf16[2,2048,768]{2,1,0:T(8,128)(2,1)} %refs_3_.9, ...), custom_call_target="tpu_custom_call" | custom-call | flops 9663676416 | bytes 23068672 | tf_op jit(solution)/shard_map/pallas_call | solution.py:68
  150.3 2.1 collective-permute-start.9
  152.4 12.5 %collective-permute-done.12 = bf16[128,2048]{1,0:T(8,128)(2,1)S(1)} collective-permute-done((bf16[128,2048]{1,0:T(8,128)(2,1)S(1)}, bf16[128,2048]{1,0:T(8,128)(2,1)S(1)}, u32[]{:S(2)}, u32[]{:S(2)}) %collective-permute-start.12) | collective-permute-done | bytes 524320 | tf_op jit(solution)/shard_map/ppermute | solution.py:131
  165.2 16.7 %shard_map.93 = (bf16[256,2048]{1,0:T(8,128)(2,1)S(1)}, bf16[256,2048]{1,0:T(8,128)(2,1)S(1)}) custom-call(bf16[256,2048]{1,0:T(8,128)(2,1)} %collective-permute-done.2.refs_0_, bf16[256,2048]{1,0:T(8,128)(2,1)} %collective-permute-done.3.refs_1_, f32[512,2]{1,0:T(8,128)S(1)} %pad_maximum_fusion.3.refs_2_, bf16[2,2048,768]{2,1,0:T(8,128)(2,1)} %refs_3_.9, ...), custom_call_target="tpu_custom_call" | custom-call | flops 9663676416 | bytes 23068672 | tf_op jit(solution)/shard_map/pallas_call | solution.py:68
  182.3 2.0 collective-permute-start.10
  184.4 4.9 %collective-permute-done.13 = bf16[256,2048]{1,0:T(8,128)(2,1)S(1)} collective-permute-done((bf16[256,2048]{1,0:T(8,128)(2,1)S(1)}, bf16[256,2048]{1,0:T(8,128)(2,1)S(1)}, u32[]{:S(2)}, u32[]{:S(2)}) %collective-permute-start.13) | collective-permute-done | bytes 1048608 | tf_op jit(solution)/shard_map/ppermute | solution.py:140
  190.0 15.7 %shard_map.92 = (bf16[256,2048]{1,0:T(8,128)(2,1)S(1)}, bf16[256,2048]{1,0:T(8,128)(2,1)S(1)}) custom-call(bf16[256,2048]{1,0:T(8,128)(2,1)S(1)} %collective-permute-done.refs_0_, bf16[256,2048]{1,0:T(8,128)(2,1)S(1)} %copy-done.2, f32[512,2]{1,0:T(8,128)S(1)} %pad_maximum_fusion.2.refs_2_, bf16[2,2048,768]{2,1,0:T(8,128)(2,1)} %refs_3_.9, ...), custom_call_target="tpu_custom_call" | custom-call | flops 9663676416 | bytes 23068672 | tf_op jit(solution)/shard_map/pallas_call | solution.py:68
  205.7 1.7 collective-permute-done.10
  207.8 2.5 %collective-permute-start.11 = (bf16[256,2048]{1,0:T(8,128)(2,1)S(1)}, bf16[256,2048]{1,0:T(8,128)(2,1)S(1)}, u32[]{:S(2)}, u32[]{:S(2)}) collective-permute-start(bf16[256,2048]{1,0:T(8,128)(2,1)S(1)} %add_convert_fusion.3), channel_id=1, source_target_pairs={{2,0},{4,2},{6,4},{7,6},{5,7},{3,5},{1,3},{0,1},{10,8},{12,10},{14... | collective-permute-start | bytes 3145736 | tf_op jit(solution)/shard_map/ppermute | solution.py:139
  210.3 4.8 %collective-permute-done.14 = bf16[256,2048]{1,0:T(8,128)(2,1)S(1)} collective-permute-done((bf16[256,2048]{1,0:T(8,128)(2,1)S(1)}, bf16[256,2048]{1,0:T(8,128)(2,1)S(1)}, u32[]{:S(2)}, u32[]{:S(2)}) %collective-permute-start.14) | collective-permute-done | bytes 1048608 | tf_op jit(solution)/shard_map/ppermute | solution.py:140
  215.6 11.3 %shard_map.91 = bf16[256,2048]{1,0:T(8,128)(2,1)S(1)} custom-call(bf16[256,2048]{1,0:T(8,128)(2,1)S(1)} %copy-done, f32[256,2]{1,0:T(8,128)S(1)} %get-tuple-element.21.refs_1_, bf16[2,2048,768]{2,1,0:T(8,128)(2,1)} %refs_3_.9, bf16[2,2048,768]{2,1,0:T(8,128)(2,1)} %refs_4_.9, bf16[2,768,2048]{2,1,0:T(8,128)(2,1)} %refs_5_.7), custom_call_target="tpu_custom_call" | custom-call | flops 4831838208 | bytes 20971520 | tf_op jit(solution)/shard_map/pallas_call | solution.py:68
  226.9 3.5 %collective-permute-done.15 = bf16[256,2048]{1,0:T(8,128)(2,1)S(1)} collective-permute-done((bf16[256,2048]{1,0:T(8,128)(2,1)S(1)}, bf16[256,2048]{1,0:T(8,128)(2,1)S(1)}, u32[]{:S(2)}, u32[]{:S(2)}) %collective-permute-start.15) | collective-permute-done | bytes 1048608 | tf_op jit(solution)/shard_map/ppermute | solution.py:140
  230.3 1.6 add_convert_fusion
  (42 shorter events, 3.2 us)
Async XLA Ops:
  0.0 26.3 %collective-permute-start = (bf16[256,2048]{1,0:T(8,128)(2,1)}, bf16[256,2048]{1,0:T(8,128)(2,1)S(1)}, u32[]{:S(2)}, u32[]{:S(2)}) collective-permute-start(bf16[256,2048]{1,0:T(8,128)(2,1)} %refs_0_.1), channel_id=1, source_target_pairs={{0,2},{2,4},{4,6},{6,7},{7,5},{5,3},{3,1},{1,0},{8,10},{10,12},{12... | collective-permute-start | bytes 3145736 | tf_op jit(solution)/shard_map/ppermute | solution.py:117
  3.0 25.1 %collective-permute-start.1 = (bf16[256,2048]{1,0:T(8,128)(2,1)}, bf16[256,2048]{1,0:T(8,128)(2,1)S(1)}, u32[]{:S(2)}, u32[]{:S(2)}) collective-permute-start(bf16[256,2048]{1,0:T(8,128)(2,1)} %refs_0_.1), channel_id=1, source_target_pairs={{2,0},{4,2},{6,4},{7,6},{5,7},{3,5},{1,3},{0,1},{10,8},{12,10},{14... | collective-permute-start | bytes 3145736 | tf_op jit(solution)/shard_map/ppermute | solution.py:118
  26.3 24.5 %collective-permute-start.2 = (bf16[256,2048]{1,0:T(8,128)(2,1)S(1)}, bf16[256,2048]{1,0:T(8,128)(2,1)}, u32[]{:S(2)}, u32[]{:S(2)}) collective-permute-start(bf16[256,2048]{1,0:T(8,128)(2,1)S(1)} %collective-permute-done.refs_0_), channel_id=1, source_target_pairs={{0,2},{2,4},{4,6},{6,7},{7,5},{5,3},{3,1},{1,0},{8,10},{10,12},{12... | collective-permute-start | bytes 3145736 | tf_op jit(solution)/shard_map/ppermute | solution.py:117
  28.1 24.1 %collective-permute-start.3 = (bf16[256,2048]{1,0:T(8,128)(2,1)S(1)}, bf16[256,2048]{1,0:T(8,128)(2,1)}, u32[]{:S(2)}, u32[]{:S(2)}) collective-permute-start(bf16[256,2048]{1,0:T(8,128)(2,1)S(1)} %collective-permute-done.1.refs_1_), channel_id=1, source_target_pairs={{2,0},{4,2},{6,4},{7,6},{5,7},{3,5},{1,3},{0,1},{10,8},{12,10},{14... | collective-permute-start | bytes 3145736 | tf_op jit(solution)/shard_map/ppermute | solution.py:118
  28.3 1.0 copy-start.1
  50.8 60.7 %collective-permute-start.4 = (bf16[256,2048]{1,0:T(8,128)(2,1)}, bf16[256,2048]{1,0:T(8,128)(2,1)S(1)}, u32[]{:S(2)}, u32[]{:S(2)}) collective-permute-start(bf16[256,2048]{1,0:T(8,128)(2,1)} %collective-permute-done.2.refs_0_), channel_id=1, source_target_pairs={{0,2},{2,4},{4,6},{6,7},{7,5},{5,3},{3,1},{1,0},{8,10},{10,12},{12... | collective-permute-start | bytes 3145736 | tf_op jit(solution)/shard_map/ppermute | solution.py:117
  52.3 59.3 %collective-permute-start.5 = (bf16[256,2048]{1,0:T(8,128)(2,1)}, bf16[256,2048]{1,0:T(8,128)(2,1)S(1)}, u32[]{:S(2)}, u32[]{:S(2)}) collective-permute-start(bf16[256,2048]{1,0:T(8,128)(2,1)} %collective-permute-done.3.refs_1_), channel_id=1, source_target_pairs={{2,0},{4,2},{6,4},{7,6},{5,7},{3,5},{1,3},{0,1},{10,8},{12,10},{14... | collective-permute-start | bytes 3145736 | tf_op jit(solution)/shard_map/ppermute | solution.py:118
  111.5 9.2 %collective-permute-start.6 = (bf16[128,2048]{1,0:T(8,128)(2,1)S(1)}, bf16[128,2048]{1,0:T(8,128)(2,1)S(1)}, u32[]{:S(2)}, u32[]{:S(2)}) collective-permute-start(bf16[128,2048]{1,0:T(8,128)(2,1)S(1)} %slice.40), channel_id=1, source_target_pairs={{0,2},{2,4},{4,6},{6,7},{7,5},{5,3},{3,1},{1,0},{8,10},{10,12},{12... | collective-permute-start | bytes 1572872 | tf_op jit(solution)/shard_map/ppermute | solution.py:122
  111.7 9.2 %collective-permute-start.7 = (bf16[128,2048]{1,0:T(8,128)(2,1)S(1)}, bf16[128,2048]{1,0:T(8,128)(2,1)S(1)}, u32[]{:S(2)}, u32[]{:S(2)}) collective-permute-start(bf16[128,2048]{1,0:T(8,128)(2,1)S(1)} %slice.41), channel_id=1, source_target_pairs={{2,0},{4,2},{6,4},{7,6},{5,7},{3,5},{1,3},{0,1},{10,8},{12,10},{14... | collective-permute-start | bytes 1572872 | tf_op jit(solution)/shard_map/ppermute | solution.py:123
  132.2 17.9 %collective-permute-start.8 = (bf16[128,2048]{1,0:T(8,128)(2,1)S(1)}, bf16[128,2048]{1,0:T(8,128)(2,1)S(1)}, u32[]{:S(2)}, u32[]{:S(2)}) collective-permute-start(bf16[128,2048]{1,0:T(8,128)(2,1)S(1)} %get-tuple-element.16), channel_id=1, source_target_pairs={{2,0},{4,2},{6,4},{7,6},{5,7},{3,5},{1,3},{0,1},{10,8},{12,10},{14... | collective-permute-start | bytes 1572872 | tf_op jit(solution)/shard_map/ppermute | solution.py:130
  150.0 14.9 %collective-permute-start.12 = (bf16[128,2048]{1,0:T(8,128)(2,1)S(1)}, bf16[128,2048]{1,0:T(8,128)(2,1)S(1)}, u32[]{:S(2)}, u32[]{:S(2)}) collective-permute-start(bf16[128,2048]{1,0:T(8,128)(2,1)S(1)} %get-tuple-element.20), channel_id=1, source_target_pairs={{0,2},{2,4},{4,6},{6,7},{7,5},{5,3},{3,1},{1,0},{8,10},{10,12},{12... | collective-permute-start | bytes 1572872 | tf_op jit(solution)/shard_map/ppermute | solution.py:131
  150.3 31.6 %collective-permute-start.9 = (bf16[256,2048]{1,0:T(8,128)(2,1)S(1)}, bf16[256,2048]{1,0:T(8,128)(2,1)S(1)}, u32[]{:S(2)}, u32[]{:S(2)}) collective-permute-start(bf16[256,2048]{1,0:T(8,128)(2,1)S(1)} %pad_maximum_fusion), channel_id=1, source_target_pairs={{2,0},{4,2},{6,4},{7,6},{5,7},{3,5},{1,3},{0,1},{10,8},{12,10},{14... | collective-permute-start | bytes 3145736 | tf_op jit(solution)/shard_map/ppermute | solution.py:139
  165.2 24.2 %collective-permute-start.13 = (bf16[256,2048]{1,0:T(8,128)(2,1)S(1)}, bf16[256,2048]{1,0:T(8,128)(2,1)S(1)}, u32[]{:S(2)}, u32[]{:S(2)}) collective-permute-start(bf16[256,2048]{1,0:T(8,128)(2,1)S(1)} %pad_maximum_fusion.1), channel_id=1, source_target_pairs={{0,2},{2,4},{4,6},{6,7},{7,5},{5,3},{3,1},{1,0},{8,10},{10,12},{12... | collective-permute-start | bytes 3145736 | tf_op jit(solution)/shard_map/ppermute | solution.py:140
  182.3 7.6 %copy-start.2 = (bf16[256,2048]{1,0:T(8,128)(2,1)S(1)}, bf16[256,2048]{1,0:T(8,128)(2,1)}, u32[]{:S(2)}) copy-start(bf16[256,2048]{1,0:T(8,128)(2,1)} %copy-done.1) | copy-start | bytes 3145732
  182.3 25.1 %collective-permute-start.10 = (bf16[256,2048]{1,0:T(8,128)(2,1)S(1)}, bf16[256,2048]{1,0:T(8,128)(2,1)S(1)}, u32[]{:S(2)}, u32[]{:S(2)}) collective-permute-start(bf16[256,2048]{1,0:T(8,128)(2,1)S(1)} %add_convert_fusion.4), channel_id=1, source_target_pairs={{2,0},{4,2},{6,4},{7,6},{5,7},{3,5},{1,3},{0,1},{10,8},{12,10},{14... | collective-permute-start | bytes 3145736 | tf_op jit(solution)/shard_map/ppermute | solution.py:139
  189.7 25.4 %collective-permute-start.14 = (bf16[256,2048]{1,0:T(8,128)(2,1)S(1)}, bf16[256,2048]{1,0:T(8,128)(2,1)S(1)}, u32[]{:S(2)}, u32[]{:S(2)}) collective-permute-start(bf16[256,2048]{1,0:T(8,128)(2,1)S(1)} %add_convert_fusion.2), channel_id=1, source_target_pairs={{0,2},{2,4},{4,6},{6,7},{7,5},{5,3},{3,1},{1,0},{8,10},{10,12},{12... | collective-permute-start | bytes 3145736 | tf_op jit(solution)/shard_map/ppermute | solution.py:140
  207.8 7.8 %copy-start = (bf16[256,2048]{1,0:T(8,128)(2,1)S(1)}, bf16[256,2048]{1,0:T(8,128)(2,1)}, u32[]{:S(2)}) copy-start(bf16[256,2048]{1,0:T(8,128)(2,1)} %refs_0_.1) | copy-start | bytes 3145732
  207.8 19.1 %collective-permute-start.11 = (bf16[256,2048]{1,0:T(8,128)(2,1)S(1)}, bf16[256,2048]{1,0:T(8,128)(2,1)S(1)}, u32[]{:S(2)}, u32[]{:S(2)}) collective-permute-start(bf16[256,2048]{1,0:T(8,128)(2,1)S(1)} %add_convert_fusion.3), channel_id=1, source_target_pairs={{2,0},{4,2},{6,4},{7,6},{5,7},{3,5},{1,3},{0,1},{10,8},{12,10},{14... | collective-permute-start | bytes 3145736 | tf_op jit(solution)/shard_map/ppermute | solution.py:139
  215.5 14.9 %collective-permute-start.15 = (bf16[256,2048]{1,0:T(8,128)(2,1)S(1)}, bf16[256,2048]{1,0:T(8,128)(2,1)S(1)}, u32[]{:S(2)}, u32[]{:S(2)}) collective-permute-start(bf16[256,2048]{1,0:T(8,128)(2,1)S(1)} %add_convert_fusion.1), channel_id=1, source_target_pairs={{0,2},{2,4},{4,6},{6,7},{7,5},{5,3},{3,1},{1,0},{8,10},{10,12},{12... | collective-permute-start | bytes 3145736 | tf_op jit(solution)/shard_map/ppermute | solution.py:140

commit v2 on v0

v2 whole, which is shorter than its diff:
```python
import functools

import jax
import jax.numpy as jnp
from jax import lax
from jax.experimental import pallas as pl
from jax.experimental.pallas import tpu as pltpu
from jax.sharding import PartitionSpec as P

VMEM_LIMIT = 48 * 1024 * 1024


def ring_order(groups):
    columns = 1 << ((groups.bit_length() - 1) // 2)
    rows = groups // columns
    walk = [z * columns for z in range(rows)]
    for turn, z in enumerate(reversed(range(rows))):
        row = [z * columns + x for x in range(1, columns)]
        walk += row if turn % 2 == 0 else row[::-1]
    return walk


def table_rows(slots, height, width):
    one = -(-slots * height // width)
    return one, -(-2 * one // 8) * 8


def pack_kernel(slots, tokens_ref, target_ref, weight_ref, out_ref):
    half, width = out_ref.shape[0], out_ref.shape[1]
    height = tokens_ref.shape[0]
    half = height // 2
    one, extra = table_rows(slots, height, width)
    per_row = width // height
    out_ref[:half, :] = tokens_ref[:half, :]
    weight = weight_ref[...]
    share = weight / jnp.sum(weight, axis=0, keepdims=True)
    target = target_ref[...]
    row = lax.broadcasted_iota(jnp.int32, (extra, height), 0)
    for lane in range(per_row):
        block = jnp.zeros((extra, height), jnp.float32)
        for r in range(one):
            slot = r * per_row + lane
            if slot < slots:
                value = jnp.sum(jnp.where(target == slot, share, 0.0), axis=0, keepdims=True)
                high = value.astype(jnp.bfloat16).astype(jnp.float32)
                block = jnp.where(row == r, high, block)
                block = jnp.where(row == one + r, value - high, block)
        out_ref[half:, lane * height:(lane + 1) * height] = block.astype(jnp.bfloat16)


def pack(tokens, target, router_weight, slots):
    height, width = tokens.shape
    extra = table_rows(slots, height, width)[1]
    return pl.pallas_call(
        functools.partial(pack_kernel, slots),
        out_shape=jax.ShapeDtypeStruct((height // 2 + extra, width), jnp.bfloat16),
        compiler_params=pltpu.CompilerParams(vmem_limit_bytes=VMEM_LIMIT),
    )(tokens, target.T, router_weight.T)


def expert_kernel(plan, place_ref, *refs):
    tiles, steps, parts, tables, slots, height = plan
    count = len(parts)
    chunks = refs[:count]
    table_refs = refs[count:count + tables]
    gate_ref, up_ref, down_ref = refs[count + tables:count + tables + 3]
    outs = refs[count + tables + 3:2 * count + tables + 3]
    rows_ref, hidden_ref, share_ref = refs[2 * count + tables + 3:]
    step = pl.program_id(0)
    half = height // 2
    width = rows_ref.shape[1]
    tile = gate_ref.shape[2]
    owned = hidden_ref.shape[1] // (tile * tiles)

    @pl.when(step == 0)
    def _():
        one, extra = table_rows(slots, height, width)
        per_row = width // height
        me, after, pick = place_ref[0], place_ref[1], place_ref[2]

        def column(ref, slot):
            lane = pl.multiple_of(lax.rem(slot, per_row) * height, height)
            block = ref[half:half + extra, pl.ds(lane, height)].astype(jnp.float32)
            row = lax.broadcasted_iota(jnp.int32, block.shape, 0)
            line = lax.div(slot, per_row)
            return jnp.sum(jnp.where((row == line) | (row == one + line), block, 0.0), axis=0, keepdims=True)

        columns = []
        for ref in table_refs:
            lent = column(ref, after * (owned + 1) + owned)
            lines = [column(ref, me * (owned + 1) + e) + jnp.where(pick == e, lent, 0.0) for e in range(owned)]
            row = lax.broadcasted_iota(jnp.int32, (128, height), 0)
            block = jnp.zeros((128, height), jnp.float32)
            for e in range(owned):
                block = jnp.where(row == e, lines[e], block)
            columns.append(block.T)
        for i, (which, first) in enumerate(parts):
            rows_ref[i * half:(i + 1) * half, :] = chunks[i][:half, :]
            share_ref[i * half:(i + 1) * half, :] = columns[which][first:first + half, :]

    @pl.when(step < steps)
    def _():
        x = rows_ref[...]
        gate = jnp.dot(x, gate_ref[0], preferred_element_type=jnp.float32)
        upper = jnp.dot(x, up_ref[0], preferred_element_type=jnp.float32)
        share = share_ref[...]
        lane = lax.broadcasted_iota(jnp.int32, share.shape, 1)
        share = jnp.sum(jnp.where(lane == step // tiles, share, 0.0), axis=1, keepdims=True)
        hidden = gate / (1.0 + jnp.exp(-gate)) * upper * share
        hidden_ref[:, pl.ds(pl.multiple_of(step * tile, tile), tile)] = hidden.astype(jnp.bfloat16)

    @pl.when(step >= steps)
    def _():
        part = jnp.dot(hidden_ref[...], down_ref[...], preferred_element_type=jnp.float32)
        for i in range(count):
            outs[i][...] = part[i * half:(i + 1) * half].astype(jnp.bfloat16)


def experts(place, chunks, tables, parts, slots, height, w_gate, w_up, w_down):
    count, half = len(chunks), height // 2
    owned, width, units = w_gate.shape
    tile = units
    tiles = units // tile
    steps = owned * tiles
    wide = width // 2
    rows = count * half
    last = steps - 1

    def whole(a):
        return pl.BlockSpec(a.shape, lambda j, place: (0, 0))

    def projection(j, place):
        at = jnp.minimum(j, last)
        return at // tiles, 0, at % tiles

    def across(j, place):
        return 0, jnp.maximum(j - steps, 0)

    flops = 6 * rows * width * units * owned
    moved = 2 * 3 * owned * width * units + 4 * rows * width
    return pl.pallas_call(
        functools.partial(expert_kernel, (tiles, steps, parts, len(tables), slots, height)),
        grid_spec=pltpu.PrefetchScalarGridSpec(
            num_scalar_prefetch=1,
            grid=(steps + width // wide,),
            in_specs=[whole(a) for a in chunks] + [whole(a) for a in tables] + [
                pl.BlockSpec((1, width, tile), projection),
                pl.BlockSpec((1, width, tile), projection),
                pl.BlockSpec((owned * units, wide), across),
            ],
            out_specs=[pl.BlockSpec((half, wide), across)] * count,
            scratch_shapes=[
                pltpu.VMEM((rows, width), jnp.bfloat16),
                pltpu.VMEM((rows, owned * units), jnp.bfloat16),
                pltpu.VMEM((rows, 128), jnp.float32),
            ],
        ),
        out_shape=[jax.ShapeDtypeStruct((half, width), jnp.bfloat16)] * count,
        compiler_params=pltpu.CompilerParams(vmem_limit_bytes=VMEM_LIMIT),
        cost_estimate=pl.CostEstimate(flops=flops, bytes_accessed=moved, transcendentals=rows * units * owned),
    )(place, *chunks, *tables, w_gate, w_up, w_down.reshape(owned * units, width))


def add(a, b):
    return (a.astype(jnp.float32) + b.astype(jnp.float32)).astype(jnp.bfloat16)


def body(tokens, target, router_weight, replica_pick, w_gate, w_up, w_down):
    height, width = tokens.shape
    half = height // 2
    groups = lax.axis_size("expert")
    slots = groups * (w_gate.shape[0] + 1)
    walk = ring_order(groups)
    ahead = [(walk[i], walk[(i + 1) % groups]) for i in range(groups)]
    back = [(b, a) for a, b in ahead]
    me = lax.axis_index("expert").astype(jnp.int32)
    after = jnp.where(me == groups - 1, 0, me + 1)
    place = jnp.stack([me, after, replica_pick[0]])
    run = functools.partial(experts, place, slots=slots, height=height, w_gate=w_gate, w_up=w_up, w_down=w_down)

    first_a = pack(tokens, target, router_weight, slots)
    first_b = tokens[half:]
    far = groups // 2
    a_left, b_left, a_right, b_right = first_a, first_b, first_a, first_b
    parts = {}
    for s in range(1, far):
        a_left = lax.ppermute(a_left, "expert", ahead)
        b_right = lax.ppermute(b_right, "expert", back)
        a_right = lax.ppermute(a_right, "expert", back)
        b_left = lax.ppermute(b_left, "expert", ahead)
        if s == 1:
            own = run([first_a, first_b], [first_a], ((0, 0), (0, half)))
        parts[s] = run([a_left, b_left, a_right, b_right], [a_left, a_right], ((0, 0), (0, half), (1, 0), (1, half)))
    a_left = lax.ppermute(a_left, "expert", ahead)
    table_right = a_right
    b_right = lax.ppermute(b_right, "expert", back)
    far_a, far_b = run([a_left, b_right], [a_left], ((0, 0), (0, half)))

    a_to_left = lax.ppermute(far_a, "expert", back)
    b_to_right = lax.ppermute(far_b, "expert", ahead)
    a_to_right = b_to_left = None
    for s in range(far - 1, 0, -1):
        pa_left, pb_left, pa_right, pb_right = parts[s]
        a_to_left = lax.ppermute(add(pa_left, a_to_left), "expert", back)
        b_to_right = lax.ppermute(add(pb_right, b_to_right), "expert", ahead)
        a_to_right = lax.ppermute(pa_right if a_to_right is None else add(pa_right, a_to_right), "expert", ahead)
        b_to_left = lax.ppermute(pb_left if b_to_left is None else add(pb_left, b_to_left), "expert", back)

    def final(own_part, x, y):
        return (own_part.astype(jnp.float32) + x.astype(jnp.float32) + y.astype(jnp.float32)).astype(jnp.bfloat16)

    return jnp.concatenate([final(own[0], a_to_left, a_to_right), final(own[1], b_to_left, b_to_right)], axis=0)


def solution(mesh):
    in_specs = (
        P(("dp", "expert"), None),
        P(("dp", "expert"), None),
        P(("dp", "expert"), None),
        P(("dp", "expert")),
        P("expert", None, None),
        P("expert", None, None),
        P("expert", None, None),
    )
    out_specs = P(("dp", "expert"), None)
    return jax.shard_map(body, mesh=mesh, in_specs=in_specs, out_specs=out_specs, check_vma=False)
```

time: 718 us -> 202 us (0.28); the launches traced: 709 us -> 202 us
  waiting for transfers between devices: 544 us -> 93.6 us
  Pallas kernels: 0 us -> 70.5 us
  matrix products: 56.2 us -> 0 us
  local copies, waits for them, and re-layouts: 55.5 us -> 2.65 us
  other arithmetic: 30.7 us -> 2.93 us
  starting transfers between devices: 21.4 us -> 31.6 us
    all_to_all x2 -> x0, waiting for transfers between devices: 544 us -> none  [the longest x1 272 us: body(): lax.all_to_all(outgoing, 'expert', split_axis=0, concat_axis=0, tiled=True)]
    ppermute x0 -> x28, waiting for transfers between devices: none -> 93.6 us  [the longest x4 28.7 us: body(): b_right = lax.ppermute(b_right, 'expert', back)]
    pallas_call x0 -> x6, Pallas kernels: none -> 70.5 us  [the longest x5 70.3 us: experts(): pl.pallas_call(functools.partial(expert_kernel, (tiles, steps, parts, len...]
    dot_general x4 -> x0, matrix products: 56.2 us -> none  [the longest x1 22.2 us: body(): jnp.einsum('nscf,sfd->nscd', hidden, w_down, preferred_element_type=jnp.f...]
    ppermute x0 -> x28, starting transfers between devices: none -> 31.6 us  [the longest x4 7.26 us: body(): b_right = lax.ppermute(b_right, 'expert', back)]
    gather x1 -> x0, local copies, waits for them, and re-layouts: 22.6 us -> none  [body(): returned.reshape(virtual * capacity, width)[row_index]]
    all_to_all x2 -> x0, starting transfers between devices: 21.4 us -> none  [the longest x1 13.8 us: body(): lax.all_to_all(results, 'expert', split_axis=0, concat_axis=0, tiled=True)]
    scatter x1 -> x0, local copies, waits for them, and re-layouts: 19 us -> none  [body(): buffer.at[row_index]]
  transfers between devices with their start and end apart: 2 -> 28, of which waited for: 2 -> 11; matrix products, arithmetic and copies ran while one was open for 0% -> 1% of each run, Pallas kernels for 0% -> 35%
where the time goes in v2:
time: 202 us
  waiting for transfers between devices  93.6 us (46%)
  Pallas kernels  70.5 us (35%)
  starting transfers between devices  31.6 us (16%)
  other arithmetic  2.93 us (1%)
  local copies, waits for them, and re-layouts  2.65 us (1%)
    pallas_call x5, Pallas kernels, experts(): pl.pallas_call(functools.partial(expert_kernel, (tiles, steps, parts, len...  70.3 us
    ppermute x4, waiting for transfers between devices, body(): b_right = lax.ppermute(b_right, 'expert', back)  28.7 us
    ppermute x3, waiting for transfers between devices, body(): a_right = lax.ppermute(a_right, 'expert', back)  16 us
    ppermute x3, waiting for transfers between devices, body(): a_to_left = lax.ppermute(add(pa_left, a_to_left), 'expert', back)  15.4 us
    ppermute x3, waiting for transfers between devices, body(): b_to_right = lax.ppermute(add(pb_right, b_to_right), 'expert', ahead)  12.1 us
    ppermute x1, waiting for transfers between devices, body(): a_to_left = lax.ppermute(far_a, 'expert', back)  10.4 us
    ppermute x1, waiting for transfers between devices, body(): b_to_right = lax.ppermute(far_b, 'expert', ahead)  8.25 us
    ppermute x4, starting transfers between devices, body(): b_right = lax.ppermute(b_right, 'expert', back)  7.26 us
  transfers between devices with their start and end apart: 28, of which 11 were waited for; matrix products, arithmetic and copies ran while one was open for 1% of the time, Pallas kernels for 35%

profile of v2, /device:TPU:0, one launch (start us, length us, event | category | flops | bytes accessed | tf_op | source)
XLA Modules:
  0.0 202.1 jit_solution(14031765242989734302)
XLA Ops:
  0.0 1.2 copy-done
  2.8 3.0 %collective-permute-start.2 = (bf16[136,2048]{1,0:T(8,128)(2,1)S(1)}, bf16[136,2048]{1,0:T(8,128)(2,1)S(1)}, u32[]{:S(2)}, u32[]{:S(2)}) collective-permute-start(bf16[136,2048]{1,0:T(8,128)(2,1)S(1)} %shard_map.73.refs_0_.refs_2_), channel_id=1, source_target_pairs={{2,0},{4,2},{6,4},{7,6},{5,7},{3,5},{1,3},{0,1},{10,8},{12,10},{14... | collective-permute-start | bytes 1671176 | tf_op jit(solution)/shard_map/ppermute | solution.py:189
  5.9 1.9 collective-permute-start.3
  8.0 11.3 %collective-permute-done.2.refs_2_.refs_5_ = bf16[136,2048]{1,0:T(8,128)(2,1)S(1)} collective-permute-done((bf16[136,2048]{1,0:T(8,128)(2,1)S(1)}, bf16[136,2048]{1,0:T(8,128)(2,1)S(1)}, u32[]{:S(2)}, u32[]{:S(2)}) %collective-permute-start.2) | collective-permute-done | bytes 557088 | tf_op jit(solution)/shard_map/ppermute | solution.py:189
  19.3 2.0 collective-permute-start.6
  21.4 9.2 %collective-permute-done.3.refs_3_ = bf16[128,2048]{1,0:T(8,128)(2,1)} collective-permute-done((bf16[128,2048]{1,0:T(8,128)(2,1)S(1)}, bf16[128,2048]{1,0:T(8,128)(2,1)}, u32[]{:S(2)}, u32[]{:S(2)}) %collective-permute-start.3) | collective-permute-done | bytes 524320 | tf_op jit(solution)/shard_map/ppermute | solution.py:188
  30.6 2.0 collective-permute-start.7
  33.5 19.5 %collective-permute-done.7.refs_3_ = bf16[128,2048]{1,0:T(8,128)(2,1)} collective-permute-done((bf16[128,2048]{1,0:T(8,128)(2,1)}, bf16[128,2048]{1,0:T(8,128)(2,1)}, u32[]{:S(2)}, u32[]{:S(2)}) %collective-permute-start.7) | collective-permute-done | bytes 524320 | tf_op jit(solution)/shard_map/ppermute | solution.py:188
  53.0 1.7 collective-permute-start.11
  55.0 1.7 collective-permute-start.10
  57.0 16.4 %shard_map.75 = (bf16[128,2048]{1,0:T(8,128)(2,1)S(1)}, bf16[128,2048]{1,0:T(8,128)(2,1)S(1)}, bf16[128,2048]{1,0:T(8,128)(2,1)S(1)}, bf16[128,2048]{1,0:T(8,128)(2,1)S(1)}) custom-call(s32[3]{0:T(128)S(1)} %pad_add_fusion.place_ref, bf16[136,2048]{1,0:T(8,128)(2,1)S(1)} %collective-permute-done.refs_0_.refs_4_, ...), custom_call_target="tpu_custom_call" | custom-call | flops 9663676416 | bytes 23068672 | tf_op jit(solution)/shard_map/pallas_call | solution.py:141
  73.5 1.7 collective-permute-start.13
  75.2 4.8 %collective-permute-done.10.refs_2_.refs_5_ = bf16[136,2048]{1,0:T(8,128)(2,1)S(1)} collective-permute-done((bf16[136,2048]{1,0:T(8,128)(2,1)S(1)}, bf16[136,2048]{1,0:T(8,128)(2,1)S(1)}, u32[]{:S(2)}, u32[]{:S(2)}) %collective-permute-start.10) | collective-permute-done | bytes 557088 | tf_op jit(solution)/shard_map/ppermute | solution.py:189
  80.0 15.3 %shard_map.77 = (bf16[128,2048]{1,0:T(8,128)(2,1)S(1)}, bf16[128,2048]{1,0:T(8,128)(2,1)S(1)}, bf16[128,2048]{1,0:T(8,128)(2,1)S(1)}, bf16[128,2048]{1,0:T(8,128)(2,1)S(1)}) custom-call(s32[3]{0:T(128)S(1)} %pad_add_fusion.place_ref, bf16[136,2048]{1,0:T(8,128)(2,1)S(1)} %collective-permute-done.8.refs_0_.refs_4_, ...), custom_call_target="tpu_custom_call" | custom-call | flops 9663676416 | bytes 23068672 | tf_op jit(solution)/shard_map/pallas_call | solution.py:141
  95.3 1.8 collective-permute-start.18
  97.1 1.6 collective-permute-start.12
  98.7 16.4 %shard_map.76 = (bf16[128,2048]{1,0:T(8,128)(2,1)S(1)}, bf16[128,2048]{1,0:T(8,128)(2,1)S(1)}, bf16[128,2048]{1,0:T(8,128)(2,1)S(1)}, bf16[128,2048]{1,0:T(8,128)(2,1)S(1)}) custom-call(s32[3]{0:T(128)S(1)} %pad_add_fusion.place_ref, bf16[136,2048]{1,0:T(8,128)(2,1)S(1)} %collective-permute-done.4.refs_0_.refs_4_, ...), custom_call_target="tpu_custom_call" | custom-call | flops 9663676416 | bytes 23068672 | tf_op jit(solution)/shard_map/pallas_call | solution.py:141
  115.6 2.6 %collective-permute-done.12.refs_0_.refs_2_ = bf16[136,2048]{1,0:T(8,128)(2,1)S(1)} collective-permute-done((bf16[136,2048]{1,0:T(8,128)(2,1)S(1)}, bf16[136,2048]{1,0:T(8,128)(2,1)S(1)}, u32[]{:S(2)}, u32[]{:S(2)}) %collective-permute-start.12) | collective-permute-done | bytes 557088 | tf_op jit(solution)/shard_map/ppermute | solution.py:194
  118.2 11.1 %shard_map.78 = (bf16[128,2048]{1,0:T(8,128)(2,1)S(1)}, bf16[128,2048]{1,0:T(8,128)(2,1)S(1)}) custom-call(s32[3]{0:T(128)S(1)} %pad_add_fusion.place_ref, bf16[136,2048]{1,0:T(8,128)(2,1)S(1)} %collective-permute-done.12.refs_0_.refs_2_, bf16[128,2048]{1,0:T(8,128)(2,1)S(1)} %collective-permute-done.13.refs_1_, ...), custom_call_target="tpu_custom_call" | custom-call | flops 4831838208 | bytes 20971520 | tf_op jit(solution)/shard_map/pallas_call | solution.py:141
  129.3 1.6 collective-permute-start.14
  133.8 10.4 %collective-permute-done.14 = bf16[128,2048]{1,0:T(8,128)(2,1)S(1)} collective-permute-done((bf16[128,2048]{1,0:T(8,128)(2,1)S(1)}, bf16[128,2048]{1,0:T(8,128)(2,1)S(1)}, u32[]{:S(2)}, u32[]{:S(2)}) %collective-permute-start.14) | collective-permute-done | bytes 524320 | tf_op jit(solution)/shard_map/ppermute | solution.py:199
  144.3 1.6 collective-permute-start.15
  146.0 8.3 %collective-permute-done.24 = bf16[128,2048]{1,0:T(8,128)(2,1)S(1)} collective-permute-done((bf16[128,2048]{1,0:T(8,128)(2,1)S(1)}, bf16[128,2048]{1,0:T(8,128)(2,1)S(1)}, u32[]{:S(2)}, u32[]{:S(2)}) %collective-permute-start.24) | collective-permute-done | bytes 524320 | tf_op jit(solution)/shard_map/ppermute | solution.py:200
  155.3 8.4 %collective-permute-done.15 = bf16[128,2048]{1,0:T(8,128)(2,1)S(1)} collective-permute-done((bf16[128,2048]{1,0:T(8,128)(2,1)S(1)}, bf16[128,2048]{1,0:T(8,128)(2,1)S(1)}, u32[]{:S(2)}, u32[]{:S(2)}) %collective-permute-start.15) | collective-permute-done | bytes 524320 | tf_op jit(solution)/shard_map/ppermute | solution.py:204
  163.8 1.6 collective-permute-start.16
  165.5 3.8 %collective-permute-done.25 = bf16[128,2048]{1,0:T(8,128)(2,1)S(1)} collective-permute-done((bf16[128,2048]{1,0:T(8,128)(2,1)S(1)}, bf16[128,2048]{1,0:T(8,128)(2,1)S(1)}, u32[]{:S(2)}, u32[]{:S(2)}) %collective-permute-start.25) | collective-permute-done | bytes 524320 | tf_op jit(solution)/shard_map/ppermute | solution.py:205
  170.0 1.6 collective-permute-start.23
  171.7 7.1 %collective-permute-done.16 = bf16[128,2048]{1,0:T(8,128)(2,1)S(1)} collective-permute-done((bf16[128,2048]{1,0:T(8,128)(2,1)S(1)}, bf16[128,2048]{1,0:T(8,128)(2,1)S(1)}, u32[]{:S(2)}, u32[]{:S(2)}) %collective-permute-start.16) | collective-permute-done | bytes 524320 | tf_op jit(solution)/shard_map/ppermute | solution.py:204
  178.9 1.6 collective-permute-start.17
  180.5 8.3 %collective-permute-done.26 = bf16[128,2048]{1,0:T(8,128)(2,1)S(1)} collective-permute-done((bf16[128,2048]{1,0:T(8,128)(2,1)S(1)}, bf16[128,2048]{1,0:T(8,128)(2,1)S(1)}, u32[]{:S(2)}, u32[]{:S(2)}) %collective-permute-start.26) | collective-permute-done | bytes 524320 | tf_op jit(solution)/shard_map/ppermute | solution.py:205
  189.4 11.1 %shard_map.74 = (bf16[128,2048]{1,0:T(8,128)(2,1)S(1)}, bf16[128,2048]{1,0:T(8,128)(2,1)S(1)}) custom-call(s32[3]{0:T(128)S(1)} %pad_add_fusion.place_ref, bf16[136,2048]{1,0:T(8,128)(2,1)S(1)} %shard_map.73.refs_0_.refs_2_, bf16[128,2048]{1,0:T(8,128)(2,1)S(1)} %slice.3.refs_1_, bf16[136,2048]{1,0:T(8,128)(2,1)S(1)} %shard_map.73.refs_0_.refs_2_, ...), custom_call_target="tpu_custom_call" | custom-call | flops 4831838208 | bytes 20971520 | tf_op jit(solution)/shard_map/pallas_call | solution.py:141
  201.0 1.1 pad_maximum_fusion
  (51 shorter events, 9.7 us)
Async XLA Ops:
  0.0 1.2 copy-start
  1.2 0.7 copy-start.1
  1.9 0.7 copy-start.2
  2.8 16.5 %collective-permute-start.2 = (bf16[136,2048]{1,0:T(8,128)(2,1)S(1)}, bf16[136,2048]{1,0:T(8,128)(2,1)S(1)}, u32[]{:S(2)}, u32[]{:S(2)}) collective-permute-start(bf16[136,2048]{1,0:T(8,128)(2,1)S(1)} %shard_map.73.refs_0_.refs_2_), channel_id=1, source_target_pairs={{2,0},{4,2},{6,4},{7,6},{5,7},{3,5},{1,3},{0,1},{10,8},{12,10},{14... | collective-permute-start | bytes 1671176 | tf_op jit(solution)/shard_map/ppermute | solution.py:189
  5.7 15.6 %collective-permute-start = (bf16[136,2048]{1,0:T(8,128)(2,1)S(1)}, bf16[136,2048]{1,0:T(8,128)(2,1)S(1)}, u32[]{:S(2)}, u32[]{:S(2)}) collective-permute-start(bf16[136,2048]{1,0:T(8,128)(2,1)S(1)} %shard_map.73.refs_0_.refs_2_), channel_id=1, source_target_pairs={{0,2},{2,4},{4,6},{6,7},{7,5},{5,3},{3,1},{1,0},{8,10},{10,12},{12... | collective-permute-start | bytes 1671176 | tf_op jit(solution)/shard_map/ppermute | solution.py:187
  5.9 24.7 %collective-permute-start.3 = (bf16[128,2048]{1,0:T(8,128)(2,1)S(1)}, bf16[128,2048]{1,0:T(8,128)(2,1)}, u32[]{:S(2)}, u32[]{:S(2)}) collective-permute-start(bf16[128,2048]{1,0:T(8,128)(2,1)S(1)} %slice.3.refs_1_), channel_id=1, source_target_pairs={{2,0},{4,2},{6,4},{7,6},{5,7},{3,5},{1,3},{0,1},{10,8},{12,10},{14... | collective-permute-start | bytes 1572872 | tf_op jit(solution)/shard_map/ppermute | solution.py:188
  7.9 24.8 %collective-permute-start.1 = (bf16[128,2048]{1,0:T(8,128)(2,1)S(1)}, bf16[128,2048]{1,0:T(8,128)(2,1)}, u32[]{:S(2)}, u32[]{:S(2)}) collective-permute-start(bf16[128,2048]{1,0:T(8,128)(2,1)S(1)} %slice.3.refs_1_), channel_id=1, source_target_pairs={{0,2},{2,4},{4,6},{6,7},{7,5},{5,3},{3,1},{1,0},{8,10},{10,12},{12... | collective-permute-start | bytes 1572872 | tf_op jit(solution)/shard_map/ppermute | solution.py:190
  19.3 35.7 %collective-permute-start.6 = (bf16[136,2048]{1,0:T(8,128)(2,1)S(1)}, bf16[136,2048]{1,0:T(8,128)(2,1)S(1)}, u32[]{:S(2)}, u32[]{:S(2)}) collective-permute-start(bf16[136,2048]{1,0:T(8,128)(2,1)S(1)} %collective-permute-done.2.refs_2_.refs_5_), channel_id=1, source_target_pairs={{2,0},{4,2},{6,4},{7,6},{5,7},{3,5},{1,3},{0,1},{10,8},{12,10},{14... | collective-permute-start | bytes 1671176 | tf_op jit(solution)/shard_map/ppermute | solution.py:189
  21.3 35.4 %collective-permute-start.4 = (bf16[136,2048]{1,0:T(8,128)(2,1)S(1)}, bf16[136,2048]{1,0:T(8,128)(2,1)S(1)}, u32[]{:S(2)}, u32[]{:S(2)}) collective-permute-start(bf16[136,2048]{1,0:T(8,128)(2,1)S(1)} %collective-permute-done.refs_0_.refs_4_), channel_id=1, source_target_pairs={{0,2},{2,4},{4,6},{6,7},{7,5},{5,3},{3,1},{1,0},{8,10},{10,12},{12... | collective-permute-start | bytes 1671176 | tf_op jit(solution)/shard_map/ppermute | solution.py:187
  30.6 22.3 %collective-permute-start.7 = (bf16[128,2048]{1,0:T(8,128)(2,1)}, bf16[128,2048]{1,0:T(8,128)(2,1)}, u32[]{:S(2)}, u32[]{:S(2)}) collective-permute-start(bf16[128,2048]{1,0:T(8,128)(2,1)} %collective-permute-done.3.refs_3_), channel_id=1, source_target_pairs={{2,0},{4,2},{6,4},{7,6},{5,7},{3,5},{1,3},{0,1},{10,8},{12,10},{14... | collective-permute-start | bytes 1572872 | tf_op jit(solution)/shard_map/ppermute | solution.py:188
  32.6 22.0 %collective-permute-start.5 = (bf16[128,2048]{1,0:T(8,128)(2,1)}, bf16[128,2048]{1,0:T(8,128)(2,1)}, u32[]{:S(2)}, u32[]{:S(2)}) collective-permute-start(bf16[128,2048]{1,0:T(8,128)(2,1)} %collective-permute-done.1.refs_1_), channel_id=1, source_target_pairs={{0,2},{2,4},{4,6},{6,7},{7,5},{5,3},{3,1},{1,0},{8,10},{10,12},{12... | collective-permute-start | bytes 1572872 | tf_op jit(solution)/shard_map/ppermute | solution.py:190
  53.0 20.5 %collective-permute-start.11 = (bf16[128,2048]{1,0:T(8,128)(2,1)}, bf16[128,2048]{1,0:T(8,128)(2,1)S(1)}, u32[]{:S(2)}, u32[]{:S(2)}) collective-permute-start(bf16[128,2048]{1,0:T(8,128)(2,1)} %collective-permute-done.7.refs_3_), channel_id=1, source_target_pairs={{2,0},{4,2},{6,4},{7,6},{5,7},{3,5},{1,3},{0,1},{10,8},{12,10},{14... | collective-permute-start | bytes 1572872 | tf_op jit(solution)/shard_map/ppermute | solution.py:188
  54.6 20.6 %collective-permute-start.9 = (bf16[128,2048]{1,0:T(8,128)(2,1)}, bf16[128,2048]{1,0:T(8,128)(2,1)S(1)}, u32[]{:S(2)}, u32[]{:S(2)}) collective-permute-start(bf16[128,2048]{1,0:T(8,128)(2,1)} %collective-permute-done.5.refs_1_), channel_id=1, source_target_pairs={{0,2},{2,4},{4,6},{6,7},{7,5},{5,3},{3,1},{1,0},{8,10},{10,12},{12... | collective-permute-start | bytes 1572872 | tf_op jit(solution)/shard_map/ppermute | solution.py:190
  55.0 25.0 %collective-permute-start.10 = (bf16[136,2048]{1,0:T(8,128)(2,1)S(1)}, bf16[136,2048]{1,0:T(8,128)(2,1)S(1)}, u32[]{:S(2)}, u32[]{:S(2)}) collective-permute-start(bf16[136,2048]{1,0:T(8,128)(2,1)S(1)} %collective-permute-done.6.refs_2_.refs_5_), channel_id=1, source_target_pairs={{2,0},{4,2},{6,4},{7,6},{5,7},{3,5},{1,3},{0,1},{10,8},{12,10},{14... | collective-permute-start | bytes 1671176 | tf_op jit(solution)/shard_map/ppermute | solution.py:189
  56.7 23.3 %collective-permute-start.8 = (bf16[136,2048]{1,0:T(8,128)(2,1)S(1)}, bf16[136,2048]{1,0:T(8,128)(2,1)S(1)}, u32[]{:S(2)}, u32[]{:S(2)}) collective-permute-start(bf16[136,2048]{1,0:T(8,128)(2,1)S(1)} %collective-permute-done.4.refs_0_.refs_4_), channel_id=1, source_target_pairs={{0,2},{2,4},{4,6},{6,7},{7,5},{5,3},{3,1},{1,0},{8,10},{10,12},{12... | collective-permute-start | bytes 1671176 | tf_op jit(solution)/shard_map/ppermute | solution.py:187
  73.5 42.1 %collective-permute-start.13 = (bf16[128,2048]{1,0:T(8,128)(2,1)S(1)}, bf16[128,2048]{1,0:T(8,128)(2,1)S(1)}, u32[]{:S(2)}, u32[]{:S(2)}) collective-permute-start(bf16[128,2048]{1,0:T(8,128)(2,1)S(1)} %collective-permute-done.11.refs_3_), channel_id=1, source_target_pairs={{2,0},{4,2},{6,4},{7,6},{5,7},{3,5},{1,3},{0,1},{10,8},{12,10},{14... | collective-permute-start | bytes 1572872 | tf_op jit(solution)/shard_map/ppermute | solution.py:196
  95.3 35.6 %collective-permute-start.18 = (bf16[128,2048]{1,0:T(8,128)(2,1)S(1)}, bf16[128,2048]{1,0:T(8,128)(2,1)S(1)}, u32[]{:S(2)}, u32[]{:S(2)}) collective-permute-start(bf16[128,2048]{1,0:T(8,128)(2,1)S(1)} %get-tuple-element.28), channel_id=1, source_target_pairs={{0,2},{2,4},{4,6},{6,7},{7,5},{5,3},{3,1},{1,0},{8,10},{10,12},{12... | collective-permute-start | bytes 1572872 | tf_op jit(solution)/shard_map/ppermute | solution.py:206
  97.1 21.1 %collective-permute-start.12 = (bf16[136,2048]{1,0:T(8,128)(2,1)S(1)}, bf16[136,2048]{1,0:T(8,128)(2,1)S(1)}, u32[]{:S(2)}, u32[]{:S(2)}) collective-permute-start(bf16[136,2048]{1,0:T(8,128)(2,1)S(1)} %collective-permute-done.8.refs_0_.refs_4_), channel_id=1, source_target_pairs={{0,2},{2,4},{4,6},{6,7},{7,5},{5,3},{3,1},{1,0},{8,10},{10,12},{12... | collective-permute-start | bytes 1671176 | tf_op jit(solution)/shard_map/ppermute | solution.py:194
  115.1 17.4 %collective-permute-start.21 = (bf16[128,2048]{1,0:T(8,128)(2,1)S(1)}, bf16[128,2048]{1,0:T(8,128)(2,1)S(1)}, u32[]{:S(2)}, u32[]{:S(2)}) collective-permute-start(bf16[128,2048]{1,0:T(8,128)(2,1)S(1)} %get-tuple-element.32), channel_id=1, source_target_pairs={{2,0},{4,2},{6,4},{7,6},{5,7},{3,5},{1,3},{0,1},{10,8},{12,10},{14... | collective-permute-start | bytes 1572872 | tf_op jit(solution)/shard_map/ppermute | solution.py:207
  129.3 14.9 %collective-permute-start.14 = (bf16[128,2048]{1,0:T(8,128)(2,1)S(1)}, bf16[128,2048]{1,0:T(8,128)(2,1)S(1)}, u32[]{:S(2)}, u32[]{:S(2)}) collective-permute-start(bf16[128,2048]{1,0:T(8,128)(2,1)S(1)} %get-tuple-element.25), channel_id=1, source_target_pairs={{2,0},{4,2},{6,4},{7,6},{5,7},{3,5},{1,3},{0,1},{10,8},{12,10},{14... | collective-permute-start | bytes 1572872 | tf_op jit(solution)/shard_map/ppermute | solution.py:199
  131.0 23.8 %collective-permute-start.19 = (bf16[128,2048]{1,0:T(8,128)(2,1)S(1)}, bf16[128,2048]{1,0:T(8,128)(2,1)S(1)}, u32[]{:S(2)}, u32[]{:S(2)}) collective-permute-start(bf16[128,2048]{1,0:T(8,128)(2,1)S(1)} %add_convert_fusion.8), channel_id=1, source_target_pairs={{0,2},{2,4},{4,6},{6,7},{7,5},{5,3},{3,1},{1,0},{8,10},{10,12},{12... | collective-permute-start | bytes 1572872 | tf_op jit(solution)/shard_map/ppermute | solution.py:206
  131.5 22.7 %collective-permute-start.24 = (bf16[128,2048]{1,0:T(8,128)(2,1)S(1)}, bf16[128,2048]{1,0:T(8,128)(2,1)S(1)}, u32[]{:S(2)}, u32[]{:S(2)}) collective-permute-start(bf16[128,2048]{1,0:T(8,128)(2,1)S(1)} %get-tuple-element.36), channel_id=1, source_target_pairs={{0,2},{2,4},{4,6},{6,7},{7,5},{5,3},{3,1},{1,0},{8,10},{10,12},{12... | collective-permute-start | bytes 1572872 | tf_op jit(solution)/shard_map/ppermute | solution.py:200
  132.7 37.2 %collective-permute-start.22 = (bf16[128,2048]{1,0:T(8,128)(2,1)S(1)}, bf16[128,2048]{1,0:T(8,128)(2,1)S(1)}, u32[]{:S(2)}, u32[]{:S(2)}) collective-permute-start(bf16[128,2048]{1,0:T(8,128)(2,1)S(1)} %add_convert_fusion.5), channel_id=1, source_target_pairs={{2,0},{4,2},{6,4},{7,6},{5,7},{3,5},{1,3},{0,1},{10,8},{12,10},{14... | collective-permute-start | bytes 1572872 | tf_op jit(solution)/shard_map/ppermute | solution.py:207
  144.3 19.4 %collective-permute-start.15 = (bf16[128,2048]{1,0:T(8,128)(2,1)S(1)}, bf16[128,2048]{1,0:T(8,128)(2,1)S(1)}, u32[]{:S(2)}, u32[]{:S(2)}) collective-permute-start(bf16[128,2048]{1,0:T(8,128)(2,1)S(1)} %add_convert_fusion.11), channel_id=1, source_target_pairs={{2,0},{4,2},{6,4},{7,6},{5,7},{3,5},{1,3},{0,1},{10,8},{12,10},{14... | collective-permute-start | bytes 1572872 | tf_op jit(solution)/shard_map/ppermute | solution.py:204
  154.4 14.9 %collective-permute-start.25 = (bf16[128,2048]{1,0:T(8,128)(2,1)S(1)}, bf16[128,2048]{1,0:T(8,128)(2,1)S(1)}, u32[]{:S(2)}, u32[]{:S(2)}) collective-permute-start(bf16[128,2048]{1,0:T(8,128)(2,1)S(1)} %add_convert_fusion.3), channel_id=1, source_target_pairs={{0,2},{2,4},{4,6},{6,7},{7,5},{5,3},{3,1},{1,0},{8,10},{10,12},{12... | collective-permute-start | bytes 1572872 | tf_op jit(solution)/shard_map/ppermute | solution.py:205
  155.0 45.5 %collective-permute-start.20 = (bf16[128,2048]{1,0:T(8,128)(2,1)S(1)}, bf16[128,2048]{1,0:T(8,128)(2,1)S(1)}, u32[]{:S(2)}, u32[]{:S(2)}) collective-permute-start(bf16[128,2048]{1,0:T(8,128)(2,1)S(1)} %add_convert_fusion.7), channel_id=1, source_target_pairs={{0,2},{2,4},{4,6},{6,7},{7,5},{5,3},{3,1},{1,0},{8,10},{10,12},{12... | collective-permute-start | bytes 1572872 | tf_op jit(solution)/shard_map/ppermute | solution.py:206
  163.8 14.9 %collective-permute-start.16 = (bf16[128,2048]{1,0:T(8,128)(2,1)S(1)}, bf16[128,2048]{1,0:T(8,128)(2,1)S(1)}, u32[]{:S(2)}, u32[]{:S(2)}) collective-permute-start(bf16[128,2048]{1,0:T(8,128)(2,1)S(1)} %add_convert_fusion.10), channel_id=1, source_target_pairs={{2,0},{4,2},{6,4},{7,6},{5,7},{3,5},{1,3},{0,1},{10,8},{12,10},{14... | collective-permute-start | bytes 1572872 | tf_op jit(solution)/shard_map/ppermute | solution.py:204
  169.4 19.4 %collective-permute-start.26 = (bf16[128,2048]{1,0:T(8,128)(2,1)S(1)}, bf16[128,2048]{1,0:T(8,128)(2,1)S(1)}, u32[]{:S(2)}, u32[]{:S(2)}) collective-permute-start(bf16[128,2048]{1,0:T(8,128)(2,1)S(1)} %add_convert_fusion.2), channel_id=1, source_target_pairs={{0,2},{2,4},{4,6},{6,7},{7,5},{5,3},{3,1},{1,0},{8,10},{10,12},{12... | collective-permute-start | bytes 1572872 | tf_op jit(solution)/shard_map/ppermute | solution.py:205
  170.0 30.7 %collective-permute-start.23 = (bf16[128,2048]{1,0:T(8,128)(2,1)S(1)}, bf16[128,2048]{1,0:T(8,128)(2,1)S(1)}, u32[]{:S(2)}, u32[]{:S(2)}) collective-permute-start(bf16[128,2048]{1,0:T(8,128)(2,1)S(1)} %add_convert_fusion.4), channel_id=1, source_target_pairs={{2,0},{4,2},{6,4},{7,6},{5,7},{3,5},{1,3},{0,1},{10,8},{12,10},{14... | collective-permute-start | bytes 1572872 | tf_op jit(solution)/shard_map/ppermute | solution.py:207
  178.9 21.6 %collective-permute-start.17 = (bf16[128,2048]{1,0:T(8,128)(2,1)S(1)}, bf16[128,2048]{1,0:T(8,128)(2,1)S(1)}, u32[]{:S(2)}, u32[]{:S(2)}) collective-permute-start(bf16[128,2048]{1,0:T(8,128)(2,1)S(1)} %add_convert_fusion.9), channel_id=1, source_target_pairs={{2,0},{4,2},{6,4},{7,6},{5,7},{3,5},{1,3},{0,1},{10,8},{12,10},{14... | collective-permute-start | bytes 1572872 | tf_op jit(solution)/shard_map/ppermute | solution.py:204
  188.9 11.9 %collective-permute-start.27 = (bf16[128,2048]{1,0:T(8,128)(2,1)S(1)}, bf16[128,2048]{1,0:T(8,128)(2,1)S(1)}, u32[]{:S(2)}, u32[]{:S(2)}) collective-permute-start(bf16[128,2048]{1,0:T(8,128)(2,1)S(1)} %add_convert_fusion.1), channel_id=1, source_target_pairs={{0,2},{2,4},{4,6},{6,7},{7,5},{5,3},{3,1},{1,0},{8,10},{10,12},{12... | collective-permute-start | bytes 1572872 | tf_op jit(solution)/shard_map/ppermute | solution.py:205
